TPU v7x, 32 devices: a whole 2x2x4 slice. The times are simulated.
32 devices in a mesh: parts: 2 (over x), lat: 16 (over z, y, core).
Axes of the slice: x: 2, y: 2, z: 4, core: 2. Of those that a mesh axis runs over, the one named last changes fastest.
Arguments:
- state: float32 [64, 512, 128], P(('parts', 'lat')), parts along dimension 0, may hold values from -6 to 6
- east_wind: float32 [64, 512, 128], P(('parts', 'lat')), parts along dimension 0, may hold values from -6 to 6
- north_wind: float32 [64, 512, 128], P(('parts', 'lat')), parts along dimension 0, may hold values from -6 to 6
- coef: float32 [64, 512], P('parts'), parts along dimension 0, may hold values from 0.5 to 2
- project: float32 [128, 128], replicated, may hold values from -0.5 to 0.5
- restore: float32 [128, 128], replicated, may hold values from -0.5 to 0.5
- stiffness: float32 [128], replicated, may hold values from 4 to 1000
- sweeps: int32 [128], replicated, may hold values from 2 to 8
- mode_slots: int32 [32, 2], P('parts'), parts along dimension 0, may hold values from -1 to 127, as said below
Outputs:
- next_state: float32 [64, 512, 128], P(('parts', 'lat')), parts along dimension 0
There are 2 independent parts, one for each index of `parts`. A program takes and returns all parts, laid end to end along the dimension named above; an argument that names none is the same for every part. Nothing has to cross between parts.
Inputs may be any that keep to these rules, and one draw needn't show every extreme that they name: `mode_slots`: row i lists the modes that device i of lat solves, -1 for an empty slot; exactly 12 distinct modes are listed in all, and some row is full.
All inputs are finite; a program needn't handle non-finite values.
Results may differ from a plain program's by a relative error of at most 0.00005.
Values sent between devices are 32-bit elements; how exact they have to be, the bound alone decides.
A program may use at most 64 MiB of HBM per device.

v0:
```python
import functools

import jax
import jax.numpy as jnp
from jax import lax
from jax.experimental import pallas as pl
from jax.experimental.pallas import tpu as pltpu
from jax.sharding import PartitionSpec as P

time_step = 0.2
diffusion = 0.05
coef_top = 2.0
sweep_limit = 8
highest = lax.Precision.HIGHEST
MESH = pl.DeviceIdType.MESH
f32 = jnp.float32
bf16 = jnp.bfloat16

REACH = sweep_limit - 1
WINDOW = 2 * REACH + 2
OFFSETS = (1, -1, 2, -2, 3, -3, 4, -4)
VMEM_LIMIT = 48 * 1024 * 1024

NN = (((1,), (0,)), ((), ()))
NT = (((1,), (1,)), ((), ()))
TN = (((0,), (0,)), ((), ()))


def split(x):
    high = x.astype(bf16)
    return high, (x - high.astype(f32)).astype(bf16)


def dot3(a, b, dims):
    (ah, al), (bh, bl) = a, b
    product = functools.partial(lax.dot_general, dimension_numbers=dims, preferred_element_type=f32)
    return product(ah, bh) + (product(ah, bl) + product(al, bh))


def kernel(devices, full, tail, state, east_wind, north_wind, coef, project, restore, stiffness, sweeps,
           mode_slots, out, sv, ev, nv, cv, pv, rv, stv, swv, msv, south, north, own, window, dir_a,
           dir_b, weight, gain, fh, fl, load_sem, halo_send, halo_recv, mode_send, mode_recv):
    me = lax.axis_index("lat")
    rows, lons, levels = state.shape
    nlat = coef.shape[0]
    half = lons // 2
    ranks = 8 * (full + tail)
    core = lax.rem(me, 2)
    chip, chips = me // 2, devices // 2

    loads = [
        pltpu.make_async_copy(source, target, load_sem.at[i])
        for i, (source, target) in enumerate((
            (state, sv), (east_wind, ev), (north_wind, nv), (project, pv), (restore, rv),
            (mode_slots, msv), (stiffness, stv), (sweeps, swv), (coef, cv)))
    ]
    for load in loads:
        load.start()

    barrier = pltpu.get_barrier_semaphore()
    for offset in OFFSETS:
        @pl.when((me + offset >= 0) & (me + offset < devices))
        def _(offset=offset):
            pl.semaphore_signal(barrier, inc=1, device_id={"lat": me + offset}, device_id_type=MESH)
    pl.semaphore_wait(barrier, jnp.minimum(me, 4) + jnp.minimum(devices - 1 - me, 4))

    def halo(way):
        return pltpu.make_async_remote_copy(
            src_ref=state.at[1 - way], dst_ref=(south, north)[way],
            send_sem=halo_send.at[way], recv_sem=halo_recv.at[way],
            device_id={"lat": me + 1 - 2 * way}, device_id_type=MESH)

    has_north = me < devices - 1
    has_south = me > 0

    @pl.when(has_north)
    def _():
        halo(0).start()

    @pl.when(has_south)
    def _():
        halo(1).start()

    @pl.when(jnp.logical_not(has_south))
    def _():
        south[...] = jnp.zeros_like(south)

    @pl.when(jnp.logical_not(has_north))
    def _():
        north[...] = jnp.zeros_like(north)

    for w in range(WINDOW):
        at = 2 * me - REACH + w

        @pl.when((at < 0) | (at >= nlat))
        def _(w=w):
            window[w] = jnp.zeros(window.shape[1:], f32)

    for load in loads[:3]:
        load.wait()
    for row in range(rows):
        here, other = sv[row], sv[1 - row]
        east = pltpu.roll(here, lons - 1, 0)
        west = pltpu.roll(here, 1, 0)
        wind = nv[row] * (0.5 * time_step)
        sign = 1.0 if row == 0 else -1.0
        ev[row] = (here - (0.5 * time_step) * ev[row] * (east - west) - sign * wind * other
                   + (time_step * diffusion) * (east + west + other - 4.0 * here))
        nv[row] = sign * wind + time_step * diffusion

    for load in loads[3:]:
        load.wait()
    number = lax.broadcasted_iota(jnp.int32, (levels, mode_slots.shape[1]), 0)
    hit = jnp.zeros(number.shape, f32)
    for slot in range(mode_slots.shape[0]):
        hit = jnp.maximum(hit, jnp.where(msv[slot:slot + 1, :] == number, 1.0, 0.0))
    hit = jnp.max(hit, axis=1, keepdims=True)
    listed = jnp.transpose(jnp.broadcast_to(hit, (levels, levels)))[0:1]
    before = lax.broadcasted_iota(jnp.int32, (levels, levels), 0) < lax.broadcasted_iota(
        jnp.int32, (levels, levels), 1)
    rank = lax.dot_general(
        jnp.broadcast_to(listed, (8, levels)).astype(bf16), jnp.where(before, 1.0, 0.0).astype(bf16),
        NN, preferred_element_type=f32)[0:1]
    place = lax.broadcasted_iota(jnp.int32, (ranks, levels), 0)
    place = jnp.where(place < 8 * full + 4, place, place - 4 * tail)
    chosen = jnp.where(rank == place.astype(f32), 1.0, 0.0) * listed
    used = jnp.sum(chosen, axis=1, keepdims=True)
    weights = jnp.sum(chosen * stv[...], axis=1, keepdims=True) + (1.0 - used)
    counts = jnp.sum(chosen * swv[...].astype(f32), axis=1, keepdims=True)
    project_sel = split(lax.dot_general(chosen, pv[...], NT, precision=highest, preferred_element_type=f32))
    restore_sel = split(lax.dot_general(chosen, rv[...], NN, precision=highest, preferred_element_type=f32))
    both = split(lax.dot_general(pv[...], rv[...], NN, precision=highest, preferred_element_type=f32))

    upper = 1.0 + weights * (coef_top * 16.0 / 3.0)
    centre = (upper + 1.0) * 0.5
    radius = (upper - 1.0) * 0.5
    ratio = centre / radius
    factor = 1.0 / ratio
    wide = (ranks, 128)
    gain[2 * REACH] = jnp.broadcast_to(1.0 / centre, wide)
    for k in range(REACH):
        next_factor = 1.0 / (2.0 * ratio - factor)
        gain[2 * k] = jnp.broadcast_to(next_factor * factor, wide)
        gain[2 * k + 1] = jnp.broadcast_to(2.0 * next_factor / radius, wide)
        factor = next_factor
    gain[2 * REACH + 1] = jnp.broadcast_to(counts, wide)
    sixth = weights / 6.0

    upper_half = lax.broadcasted_iota(jnp.int32, (8, half), 0) < 4
    groups = [(slice(8 * g, 8 * g + 8), slice(g * lons, (g + 1) * lons), False) for g in range(full)]
    if tail:
        groups.append((slice(8 * full, 8 * full + 8), slice(full * lons, full * lons + half), True))

    for w in range(1, WINDOW - 1):
        at = 2 * me - REACH + w
        inside = jnp.where((at >= 0) & (at < nlat), 1.0, 0.0)
        line = cv[pl.ds(jnp.clip(at, 0, nlat - 1), 1), :] * inside
        for part, lanes, is_tail in groups:
            if is_tail:
                weight[w - 1, :, lanes] = sixth[part] * jnp.where(upper_half, line[:, :half], line[:, half:])
            else:
                weight[w - 1, :, lanes] = sixth[part] * line

    def copy(index, source, first, count, target_row, target):
        return pltpu.make_async_remote_copy(
            src_ref=source.at[pl.ds(first, count)], dst_ref=window.at[pl.ds(target_row, count)],
            send_sem=mode_send.at[index], recv_sem=mode_recv.at[index],
            device_id={"lat": target}, device_id_type=MESH)

    sibling = me + 1 - 2 * core
    low1, low2, high1, high2 = chip >= 1, chip >= 2, chip + 1 < chips, chip + 2 < chips
    near = ((core == 0) & low2) | ((core == 1) & high2)
    far = ((core == 1) & low2) | ((core == 0) & high2)
    always = me >= 0
    sends = (
        (lambda: copy(3, own, 1, 1, 0, me + 4), high2, low2),
        (lambda: copy(4, own, 0, 1, WINDOW - 1, me - 4), low2, high2),
        (lambda: copy(5, own, 1 - core, 1, 14 - 13 * core, me - 3 + 6 * core), near, near),
        (lambda: copy(1, own, 0, 2, 3, me + 2), high1, low1),
        (lambda: copy(2, own, 0, 2, 11, me - 2), low1, high1),
        (lambda: copy(0, own, 0, 2, 5 + 4 * core, sibling), always, always),
    )
    relays = (
        (lambda: copy(6, window, 3, 2, 1 + 4 * core, sibling), low1, low1, (3,)),
        (lambda: copy(7, window, 11, 2, 9 + 4 * core, sibling), high1, high1, (4,)),
        (lambda: copy(8, window, 15 - 15 * core, 1, 13 - 11 * core, sibling), far, near, (0, 1)),
    )

    for row in range(rows):
        @pl.when((has_south, has_north)[row])
        def _(row=row):
            halo(row).wait_recv()
        forcing = ev[row] + nv[row] * (south, north)[row][...]
        pieces = split(forcing)
        fh[row], fl[row] = pieces
        modes = dot3(project_sel, pieces, NT)
        for part, lanes, is_tail in groups:
            field = modes[part]
            if is_tail:
                field = jnp.where(upper_half, field[:, :half], field[:, half:])
            own[row, :, lanes] = field
            window[REACH + row, :, lanes] = field

    for start, sent, _ in sends[3:5] + sends[:3] + sends[5:]:
        @pl.when(sent)
        def _(start=start):
            start().start()

    out[0] = dot3((fh[0], fl[0]), both, NN)
    for start, sent, _, needs in relays:
        for need in needs:
            @pl.when(sends[need][2])
            def _(need=need):
                sends[need][0]().wait_recv()

        @pl.when(sent)
        def _(start=start):
            start().start()
    out[1] = dot3((fh[1], fl[1]), both, NN)
    for start, _, received in (sends[2], sends[5]) + tuple(relay[:3] for relay in relays):
        @pl.when(received)
        def _(start=start):
            start().wait_recv()

    for start, sent in [entry[:2] for entry in relays]:
        @pl.when(sent)
        def _(start=start):
            start().wait_send()

    for part, lanes, is_tail in groups:
        lon = half if is_tail else lons

        def spread(value):
            return jnp.concatenate([value] * (lon // 128), axis=1)

        def shifted(value, by):
            moved = pltpu.roll(value, by % lon, 1)
            if not is_tail:
                return moved
            edge = lax.broadcasted_iota(jnp.int32, (8, lon), 1) == (0 if by == 1 else lon - 1)
            return jnp.where(edge, pltpu.roll(moved, 4, 0), moved)

        inverse = spread(gain[2 * REACH, part])
        limit = spread(gain[2 * REACH + 1, part])
        for w in range(WINDOW):
            dir_a[w, :, :lon] = window[w, :, lanes] * inverse
        totals = [dir_a[REACH, :, :lon], dir_a[REACH + 1, :, :lon]]
        now, later = dir_a, dir_b
        for k in range(REACH):
            keep, push = spread(gain[2 * k, part]), spread(gain[2 * k + 1, part])
            for w in range(k + 1, WINDOW - 1 - k):
                here = now[w, :, :lon]
                sides = now[w - 1, :, :lon] + now[w + 1, :, :lon]
                mixed = 4.0 * here + sides
                laplace = shifted(mixed, 1) + shifted(mixed, -1) + (4.0 * sides - 20.0 * here)
                residual = window[w, :, lanes] - (here - weight[w - 1, :, lanes] * laplace)
                if k < REACH - 1:
                    window[w, :, lanes] = residual
                fresh = keep * here + push * residual
                later[w, :, :lon] = fresh
                if REACH <= w < REACH + 2:
                    totals[w - REACH] += jnp.where(k + 1 < limit, fresh, 0.0)
            now, later = later, now
        few = tuple(piece[part] for piece in restore_sel)
        for row in range(rows):
            change = totals[row] - own[row, :, lanes]
            if is_tail:
                change = jnp.concatenate(
                    [jnp.where(upper_half, change, 0.0), jnp.where(upper_half, 0.0, change)], axis=1)
            out[row] += dot3(split(change), few, TN)

    @pl.when(has_north)
    def _():
        halo(0).wait_send()

    @pl.when(has_south)
    def _():
        halo(1).wait_send()
    for start, sent in [entry[:2] for entry in sends]:
        @pl.when(sent)
        def _(start=start):
            start().wait_send()


def solution(mesh):
    devices = mesh.shape["lat"]

    def local(state, east_wind, north_wind, coef, project, restore, stiffness, sweeps, mode_slots):
        rows, lons, levels = state.shape
        nlat = coef.shape[0]
        listed = mode_slots.shape[0] * mode_slots.shape[1] * 3 // 8
        full, rest = listed // 8, listed % 8
        tail = 1 if rest == 4 else 0
        full += 1 if rest and not tail else 0
        ranks = 8 * (full + tail)
        packed = full * lons + tail * lons // 2
        anywhere = pl.BlockSpec(memory_space=pl.ANY)
        vmem = pltpu.VMEM
        block = vmem((rows, lons, levels), f32)
        return pl.pallas_call(
            functools.partial(kernel, devices, full, tail),
            out_shape=pltpu.VMEM(state.shape, f32),
            in_specs=[anywhere] * 9,
            out_specs=pl.BlockSpec(memory_space=pltpu.VMEM),
            scratch_shapes=[
                block, block, block,
                vmem(coef.shape, f32), vmem(project.shape, f32), vmem(restore.shape, f32),
                vmem((1, levels), f32), vmem((1, levels), jnp.int32),
                vmem(mode_slots.shape[::-1], jnp.int32),
                vmem((lons, levels), f32), vmem((lons, levels), f32),
                vmem((rows, 8, packed), f32), vmem((WINDOW, 8, packed), f32),
                vmem((WINDOW, 8, lons), f32), vmem((WINDOW, 8, lons), f32),
                vmem((WINDOW - 2, 8, packed), f32), vmem((2 * REACH + 2, ranks, 128), f32),
                vmem((rows, lons, levels), bf16), vmem((rows, lons, levels), bf16),
                pltpu.SemaphoreType.DMA((9,)),
                pltpu.SemaphoreType.DMA((2,)), pltpu.SemaphoreType.DMA((2,)),
                pltpu.SemaphoreType.DMA((9,)), pltpu.SemaphoreType.DMA((9,)),
            ],
            compiler_params=pltpu.CompilerParams(
                collective_id=0, has_side_effects=True, vmem_limit_bytes=VMEM_LIMIT),
        )(state, east_wind, north_wind, coef, project, restore, stiffness.reshape(1, levels),
          sweeps.reshape(1, levels), mode_slots.T)

    placed = (
        P(("parts", "lat"), None, None),
        P(("parts", "lat"), None, None),
        P(("parts", "lat"), None, None),
        P("parts", None),
        P(),
        P(),
        P(),
        P(),
        P("parts", None),
    )
    return jax.shard_map(
        local,
        mesh=mesh,
        in_specs=placed,
        out_specs=P(("parts", "lat"), None, None),
        check_vma=False,
    )
```

profile of v0, /device:TPU:0, one launch (start us, length us, event | category | flops | bytes accessed | tf_op | source)
XLA Modules:
  0.0 25.1 jit_solution(15773190478490909045)
XLA Ops:
  0.0 0.0 copy-start.8
  0.0 0.0 copy-start.6
  0.0 0.0 copy-start.7
  0.0 0.6 %copy-done.8 = s32[128]{0:T(128)S(1)} copy-done((s32[128]{0:T(128)S(1)}, s32[128]{0:T(128)}, u32[]{:S(2)}) %copy-start.8) | copy-done | bytes 536
  0.7 0.0 copy-done.6
  0.7 0.0 copy-done.7
  0.7 0.0 copy-start
  0.7 1.0 %copy-done = f32[2,512,128]{2,1,0:T(8,128)S(1)} copy-done((f32[2,512,128]{2,1,0:T(8,128)S(1)}, f32[2,512,128]{2,1,0:T(8,128)}, u32[]{:S(2)}) %copy-start) | copy-done | bytes 524312
  1.7 0.0 copy-start.1
  1.7 1.0 %copy-done.1 = f32[2,512,128]{2,1,0:T(8,128)S(1)} copy-done((f32[2,512,128]{2,1,0:T(8,128)S(1)}, f32[2,512,128]{2,1,0:T(8,128)}, u32[]{:S(2)}) %copy-start.1) | copy-done | bytes 524312
  2.8 0.0 copy-start.2
  2.8 1.0 %copy-done.2 = f32[2,512,128]{2,1,0:T(8,128)S(1)} copy-done((f32[2,512,128]{2,1,0:T(8,128)S(1)}, f32[2,512,128]{2,1,0:T(8,128)}, u32[]{:S(2)}) %copy-start.2) | copy-done | bytes 524312
  3.8 0.0 copy-start.3
  3.8 0.8 %copy-done.3 = f32[32,512]{1,0:T(8,128)S(1)} copy-done((f32[32,512]{1,0:T(8,128)S(1)}, f32[32,512]{1,0:T(8,128)}, u32[]{:S(2)}) %copy-start.3) | copy-done | bytes 65560
  4.7 0.0 copy-start.4
  4.7 0.8 %copy-done.4 = f32[128,128]{1,0:T(8,128)S(1)} copy-done((f32[128,128]{1,0:T(8,128)S(1)}, f32[128,128]{1,0:T(8,128)}, u32[]{:S(2)}) %copy-start.4) | copy-done | bytes 65560
  5.5 0.0 copy-start.5
  5.5 0.8 %copy-done.5 = f32[128,128]{1,0:T(8,128)S(1)} copy-done((f32[128,128]{1,0:T(8,128)S(1)}, f32[128,128]{1,0:T(8,128)}, u32[]{:S(2)}) %copy-start.5) | copy-done | bytes 65560
  6.3 18.0 %shard_map.91 = f32[2,512,128]{2,1,0:T(8,128)S(1)} custom-call(f32[2,512,128]{2,1,0:T(8,128)S(1)} %copy-done, f32[2,512,128]{2,1,0:T(8,128)S(1)} %copy-done.1, f32[2,512,128]{2,1,0:T(8,128)S(1)} %copy-done.2, f32[32,512]{1,0:T(8,128)S(1)} %copy-done.3, f32[128,128]{1,0:T(8,128)S(1)} %copy-done.4, f32[128,128]{1,0:T(8,128)S(1)} %copy-done.5, ...), custom_call_target="tpu_custom_call" | custom-call | tf_op jit(solution)/shard_map/pallas_call | solution.py:300
  24.3 0.8 %copy.11 = f32[2,512,128]{2,1,0:T(8,128)} copy(f32[2,512,128]{2,1,0:T(8,128)S(1)} %shard_map.91) | data formatting | bytes 1048576
Async XLA Ops:
  0.0 0.7 %copy-start.8 = (s32[128]{0:T(128)S(1)}, s32[128]{0:T(128)}, u32[]{:S(2)}) copy-start(s32[128]{0:T(128)} %param.16) | copy-start | bytes 1540
  0.0 0.7 %copy-start.6 = (s32[16,2]{0,1:T(2,128)S(1)}, s32[16,2]{0,1:T(2,128)}, u32[]{:S(2)}) copy-start(s32[16,2]{0,1:T(2,128)} %param.17) | copy-start | bytes 388
  0.0 0.7 %copy-start.7 = (f32[128]{0:T(128)S(1)}, f32[128]{0:T(128)}, u32[]{:S(2)}) copy-start(f32[128]{0:T(128)} %param.15) | copy-start | bytes 1540
  0.7 1.0 %copy-start = (f32[2,512,128]{2,1,0:T(8,128)S(1)}, f32[2,512,128]{2,1,0:T(8,128)}, u32[]{:S(2)}) copy-start(f32[2,512,128]{2,1,0:T(8,128)} %state.1) | copy-start | bytes 1572868
  1.7 1.0 %copy-start.1 = (f32[2,512,128]{2,1,0:T(8,128)S(1)}, f32[2,512,128]{2,1,0:T(8,128)}, u32[]{:S(2)}) copy-start(f32[2,512,128]{2,1,0:T(8,128)} %east_wind.1) | copy-start | bytes 1572868
  2.8 1.0 %copy-start.2 = (f32[2,512,128]{2,1,0:T(8,128)S(1)}, f32[2,512,128]{2,1,0:T(8,128)}, u32[]{:S(2)}) copy-start(f32[2,512,128]{2,1,0:T(8,128)} %north_wind.1) | copy-start | bytes 1572868
  3.8 0.8 %copy-start.3 = (f32[32,512]{1,0:T(8,128)S(1)}, f32[32,512]{1,0:T(8,128)}, u32[]{:S(2)}) copy-start(f32[32,512]{1,0:T(8,128)} %coef.1) | copy-start | bytes 196612
  4.7 0.8 %copy-start.4 = (f32[128,128]{1,0:T(8,128)S(1)}, f32[128,128]{1,0:T(8,128)}, u32[]{:S(2)}) copy-start(f32[128,128]{1,0:T(8,128)} %project.1) | copy-start | bytes 196612
  5.5 0.8 %copy-start.5 = (f32[128,128]{1,0:T(8,128)S(1)}, f32[128,128]{1,0:T(8,128)}, u32[]{:S(2)}) copy-start(f32[128,128]{1,0:T(8,128)} %restore.1) | copy-start | bytes 196612
where the time goes:
time: 25.5 us; the launch traced here: 25.1 us
  Pallas kernels  18 us (71%)
  local copies, waits for them, and re-layouts  7.13 us (28%)
    pallas_call x1, Pallas kernels, local(): pl.pallas_call(functools.partial(kernel, devices, full, tail), out_shape=...  18 us
    unnamed x19, local copies, waits for them, and re-layouts  7.13 us

commit v1 on v0

--- a/solution.py
+++ b/solution.py
@@ -19,7 +19,7 @@
 REACH = sweep_limit - 1
 WINDOW = 2 * REACH + 2
 OFFSETS = (1, -1, 2, -2, 3, -3, 4, -4)
-VMEM_LIMIT = 48 * 1024 * 1024
+VMEM_LIMIT = 60 * 1024 * 1024
 
 NN = (((1,), (0,)), ((), ()))
 NT = (((1,), (1,)), ((), ()))

time: 25.5 us -> 18.8 us (0.74)
  local copies, waits for them, and re-layouts: 7.13 us -> 0.8 us
    unnamed x19 -> x1, local copies, waits for them, and re-layouts: 7.13 us -> 0.8 us
where the time goes in v1:
time: 18.8 us; the launch traced here: 18.6 us
  Pallas kernels  17.8 us (95%)
  local copies, waits for them, and re-layouts  0.8 us (4%)
    pallas_call x1, Pallas kernels, local(): pl.pallas_call(functools.partial(kernel, devices, full, tail), out_shape=...  17.8 us
    unnamed x1, local copies, waits for them, and re-layouts  0.8 us

profile of v1, /device:TPU:0, one launch (start us, length us, event | category | flops | bytes accessed | tf_op | source)
XLA Modules:
  0.0 18.6 jit_solution(2052997752088754847)
XLA Ops:
  0.0 17.8 %shard_map.91 = f32[2,512,128]{2,1,0:T(8,128)S(1)} custom-call(f32[2,512,128]{2,1,0:T(8,128)} %state.1, f32[2,512,128]{2,1,0:T(8,128)} %east_wind.1, f32[2,512,128]{2,1,0:T(8,128)} %north_wind.1, f32[32,512]{1,0:T(8,128)} %coef.1, f32[128,128]{1,0:T(8,128)} %project.1, f32[128,128]{1,0:T(8,128)} %restore.1, f32[1,128]{1,0:T(1,128)} %bitcast.4, ...), custom_call_target="tpu_custom_call" | custom-call | tf_op jit(solution)/shard_map/pallas_call | solution.py:300
  17.8 0.8 %copy.11 = f32[2,512,128]{2,1,0:T(8,128)} copy(f32[2,512,128]{2,1,0:T(8,128)S(1)} %shard_map.91) | data formatting | bytes 1048576

commit v2 on v1

--- a/solution.py
+++ b/solution.py
@@ -38,8 +38,8 @@
 
 
 def kernel(devices, full, tail, state, east_wind, north_wind, coef, project, restore, stiffness, sweeps,
-           mode_slots, out, sv, ev, nv, cv, pv, rv, stv, swv, msv, south, north, own, window, dir_a,
-           dir_b, weight, gain, fh, fl, load_sem, halo_send, halo_recv, mode_send, mode_recv):
+           mode_slots, out, sv, ev, nv, cv, pv, rv, stv, swv, msv, outer_halo, inner_halo, own, window, dir_a,
+           dir_b, left, weight, gain, fh, fl, load_sem, halo_send, halo_recv, mode_send, mode_recv):
     me = lax.axis_index("lat")
     rows, lons, levels = state.shape
     nlat = coef.shape[0]
@@ -47,6 +47,11 @@
     ranks = 8 * (full + tail)
     core = lax.rem(me, 2)
     chip, chips = me // 2, devices // 2
+    tiles = lons // 128
+    chunks = tiles // 2
+    width = (2 * full + tail) * 128
+    packed = chunks * width
+    inner, outer = 1 - core, core
 
     loads = [
         pltpu.make_async_copy(source, target, load_sem.at[i])
@@ -64,30 +69,36 @@
             pl.semaphore_signal(barrier, inc=1, device_id={"lat": me + offset}, device_id_type=MESH)
     pl.semaphore_wait(barrier, jnp.minimum(me, 4) + jnp.minimum(devices - 1 - me, 4))
 
-    def halo(way):
+    low1, low2, high1, high2 = chip >= 1, chip >= 2, chip + 1 < chips, chip + 2 < chips
+    is0, is1 = core == 0, core == 1
+    always = me >= 0
+    sibling = me + 1 - 2 * core
+    beyond = me - 1 + 2 * core
+    has_beyond = (is0 & low1) | (is1 & high1)
+
+    def halo(tile):
+        span = pl.ds(tile * 128, 128)
         return pltpu.make_async_remote_copy(
-            src_ref=state.at[1 - way], dst_ref=(south, north)[way],
-            send_sem=halo_send.at[way], recv_sem=halo_recv.at[way],
-            device_id={"lat": me + 1 - 2 * way}, device_id_type=MESH)
-
-    has_north = me < devices - 1
-    has_south = me > 0
-
-    @pl.when(has_north)
+            src_ref=state.at[outer, span], dst_ref=outer_halo.at[span],
+            send_sem=halo_send.at[tile], recv_sem=halo_recv.at[tile],
+            device_id={"lat": beyond}, device_id_type=MESH)
+
+    between = pltpu.make_async_remote_copy(
+        src_ref=state.at[inner], dst_ref=inner_halo,
+        send_sem=halo_send.at[tiles], recv_sem=halo_recv.at[tiles],
+        device_id={"lat": sibling}, device_id_type=MESH)
+
+    @pl.when(has_beyond)
     def _():
-        halo(0).start()
-
-    @pl.when(has_south)
+        for chunk in range(chunks):
+            halo(chunk).start()
+            halo(chunk + chunks).start()
+
+    between.start()
+
+    @pl.when(jnp.logical_not(has_beyond))
     def _():
-        halo(1).start()
-
-    @pl.when(jnp.logical_not(has_south))
-    def _():
-        south[...] = jnp.zeros_like(south)
-
-    @pl.when(jnp.logical_not(has_north))
-    def _():
-        north[...] = jnp.zeros_like(north)
+        outer_halo[...] = jnp.zeros_like(outer_halo)
 
     for w in range(WINDOW):
         at = 2 * me - REACH + w
@@ -98,15 +109,15 @@
 
     for load in loads[:3]:
         load.wait()
-    for row in range(rows):
+    sign0 = (0.5 * time_step) * (2 * core - 1).astype(f32)
+    for row, sign in ((inner, sign0), (outer, -sign0)):
         here, other = sv[row], sv[1 - row]
         east = pltpu.roll(here, lons - 1, 0)
         west = pltpu.roll(here, 1, 0)
-        wind = nv[row] * (0.5 * time_step)
-        sign = 1.0 if row == 0 else -1.0
-        ev[row] = (here - (0.5 * time_step) * ev[row] * (east - west) - sign * wind * other
+        wind = nv[row] * sign
+        ev[row] = (here - (0.5 * time_step) * ev[row] * (east - west) - wind * other
                    + (time_step * diffusion) * (east + west + other - 4.0 * here))
-        nv[row] = sign * wind + time_step * diffusion
+        nv[row] = wind + time_step * diffusion
 
     for load in loads[3:]:
         load.wait()
@@ -147,87 +158,136 @@
     sixth = weights / 6.0
 
     upper_half = lax.broadcasted_iota(jnp.int32, (8, half), 0) < 4
-    groups = [(slice(8 * g, 8 * g + 8), slice(g * lons, (g + 1) * lons), False) for g in range(full)]
+    upper_tile = lax.broadcasted_iota(jnp.int32, (8, 128), 0) < 4
+    groups = [(g, slice(8 * g, 8 * g + 8), slice(g * lons, (g + 1) * lons), False) for g in range(full)]
     if tail:
-        groups.append((slice(8 * full, 8 * full + 8), slice(full * lons, full * lons + half), True))
+        groups.append((full, slice(8 * full, 8 * full + 8), slice(full * lons, full * lons + half), True))
+
+    def place_of(g, tile):
+        first = (tile % chunks) * width + (2 * g + tile // chunks) * 128
+        return slice(first, first + 128)
+
+    def gather(ref, row, g, is_tail):
+        return jnp.concatenate(
+            [ref[row, :, place_of(g, tile)] for tile in range(chunks if is_tail else tiles)], axis=1)
 
     for w in range(1, WINDOW - 1):
         at = 2 * me - REACH + w
         inside = jnp.where((at >= 0) & (at < nlat), 1.0, 0.0)
         line = cv[pl.ds(jnp.clip(at, 0, nlat - 1), 1), :] * inside
-        for part, lanes, is_tail in groups:
+        for _, part, lanes, is_tail in groups:
             if is_tail:
                 weight[w - 1, :, lanes] = sixth[part] * jnp.where(upper_half, line[:, :half], line[:, half:])
             else:
                 weight[w - 1, :, lanes] = sixth[part] * line
 
-    def copy(index, source, first, count, target_row, target):
+    def copy(send, recv, source, row, first, size, w, target):
+        lanes = pl.ds(first, size)
         return pltpu.make_async_remote_copy(
-            src_ref=source.at[pl.ds(first, count)], dst_ref=window.at[pl.ds(target_row, count)],
-            send_sem=mode_send.at[index], recv_sem=mode_recv.at[index],
+            src_ref=source.at[pl.ds(row, 1), :, lanes], dst_ref=window.at[pl.ds(w, 1), :, lanes],
+            send_sem=mode_send.at[send], recv_sem=mode_recv.at[recv],
             device_id={"lat": target}, device_id_type=MESH)
 
-    sibling = me + 1 - 2 * core
-    low1, low2, high1, high2 = chip >= 1, chip >= 2, chip + 1 < chips, chip + 2 < chips
-    near = ((core == 0) & low2) | ((core == 1) & high2)
-    far = ((core == 1) & low2) | ((core == 0) & high2)
-    always = me >= 0
-    sends = (
-        (lambda: copy(3, own, 1, 1, 0, me + 4), high2, low2),
-        (lambda: copy(4, own, 0, 1, WINDOW - 1, me - 4), low2, high2),
-        (lambda: copy(5, own, 1 - core, 1, 14 - 13 * core, me - 3 + 6 * core), near, near),
-        (lambda: copy(1, own, 0, 2, 3, me + 2), high1, low1),
-        (lambda: copy(2, own, 0, 2, 11, me - 2), low1, high1),
-        (lambda: copy(0, own, 0, 2, 5 + 4 * core, sibling), always, always),
+    def whole(send, recv, w, target, source=own, row=inner):
+        return lambda: copy(send, recv, source, row, 0, packed, w, target)
+
+    def piece(chunk, send, recv, w, target):
+        base = 9 + 7 * chunk
+        return lambda: copy(base + send, base + recv, own, outer, chunk * width, width, w, target)
+
+    inner_sends = (
+        (whole(1, 1, 4 - core, me + 2), high1),
+        (whole(2, 2, 12 - core, me - 2), low1),
+        (whole(3, 3 + core, core, me + 4 - core), high2),
+        (whole(5, 5 + core, 14 + core, me - 3 - core), low2),
+        (whole(0, 0, 6 + 3 * core, sibling), always),
+    )
+    first_hops = (
+        (whole(1, 1, 4 - core, sibling), low1),
+        (whole(2, 2, 12 - core, sibling), high1),
     )
     relays = (
-        (lambda: copy(6, window, 3, 2, 1 + 4 * core, sibling), low1, low1, (3,)),
-        (lambda: copy(7, window, 11, 2, 9 + 4 * core, sibling), high1, high1, (4,)),
-        (lambda: copy(8, window, 15 - 15 * core, 1, 13 - 11 * core, sibling), far, near, (0, 1)),
-    )
-
-    for row in range(rows):
-        @pl.when((has_south, has_north)[row])
-        def _(row=row):
-            halo(row).wait_recv()
-        forcing = ev[row] + nv[row] * (south, north)[row][...]
-        pieces = split(forcing)
-        fh[row], fl[row] = pieces
-        modes = dot3(project_sel, pieces, NT)
-        for part, lanes, is_tail in groups:
-            field = modes[part]
+        (whole(7, 7, 2 + 3 * core, sibling, window, 4 - core), low1),
+        (whole(8, 8, 10 + 3 * core, sibling, window, 12 - core), high1),
+    )
+    inner_arrivals = (
+        (whole(0, 0, 9 - 3 * core, sibling), always),
+        (whole(3, 3, 0, sibling), is0 & low2),
+        (whole(4, 4, 1, sibling), is0 & low2),
+        (whole(5, 5, 14, sibling), is1 & high2),
+        (whole(6, 6, 15, sibling), is1 & high2),
+        (whole(7, 7, 5 - 3 * core, sibling), low1),
+        (whole(8, 8, 13 - 3 * core, sibling), high1),
+    )
+
+    def outer_sends(chunk):
+        far, far_w = me - 4 + 7 * core, 15 - 13 * core
+        far_on = (is1 & high2) | (is0 & low2)
+        return tuple(
+            entry for to in range(2) for entry in (
+                (piece(chunk, 1 + to, 1 + core, 3 + 3 * core - 2 * to, me - core + 2 + to), high1),
+                (piece(chunk, 3 + to, 3 + core, 11 + 3 * core - 2 * to, me - core - 2 + to), low1),
+                (piece(chunk, 5 + to, 6 - core, far_w - 2 * to, far + to), far_on),
+            )) + ((piece(chunk, 0, 0, 5 + 5 * core, sibling), always),)
+
+    def outer_arrivals(chunk):
+        return tuple(
+            entry for by in range(2) for entry in (
+                (piece(chunk, 1 + by, 1 + by, 3 + 3 * by - 2 * core, sibling), low1),
+                (piece(chunk, 3 + by, 3 + by, 11 + 3 * by - 2 * core, sibling), high1),
+            )) + (
+                (piece(chunk, 0, 0, 10 - 5 * core, sibling), always),
+                (piece(chunk, 5, 5, 2 - 2 * core, sibling), low2),
+                (piece(chunk, 6, 6, 15 - 2 * core, sibling), high2),
+            )
+
+    def each(entries, action):
+        for make, on in entries:
+            @pl.when(on)
+            def _(make=make):
+                getattr(make(), action)()
+
+    def project_tiles(row, chunk, halo_ref, ready):
+        found = []
+        for tile in (chunk, chunk + chunks):
+            ready(tile)
+            span = pl.ds(tile * 128, 128)
+            forcing = ev[row, span] + nv[row, span] * halo_ref[span]
+            pieces = split(forcing)
+            fh[row, span], fl[row, span] = pieces
+            found.append(dot3(project_sel, pieces, NT))
+        for g, part, _, is_tail in groups:
             if is_tail:
-                field = jnp.where(upper_half, field[:, :half], field[:, half:])
-            own[row, :, lanes] = field
-            window[REACH + row, :, lanes] = field
-
-    for start, sent, _ in sends[3:5] + sends[:3] + sends[5:]:
-        @pl.when(sent)
-        def _(start=start):
-            start().start()
-
-    out[0] = dot3((fh[0], fl[0]), both, NN)
-    for start, sent, _, needs in relays:
-        for need in needs:
-            @pl.when(sends[need][2])
-            def _(need=need):
-                sends[need][0]().wait_recv()
-
-        @pl.when(sent)
-        def _(start=start):
-            start().start()
-    out[1] = dot3((fh[1], fl[1]), both, NN)
-    for start, _, received in (sends[2], sends[5]) + tuple(relay[:3] for relay in relays):
-        @pl.when(received)
-        def _(start=start):
-            start().wait_recv()
-
-    for start, sent in [entry[:2] for entry in relays]:
-        @pl.when(sent)
-        def _(start=start):
-            start().wait_send()
-
-    for part, lanes, is_tail in groups:
+                fields = ((chunk, jnp.where(upper_tile, found[0][part], found[1][part])),)
+            else:
+                fields = ((chunk, found[0][part]), (chunk + chunks, found[1][part]))
+            for tile, field in fields:
+                own[row, :, place_of(g, tile)] = field
+                window[REACH + row, :, place_of(g, tile)] = field
+
+    between.wait_recv()
+    for chunk in range(chunks):
+        project_tiles(inner, chunk, inner_halo, lambda tile: None)
+    out[inner] = dot3((fh[inner], fl[inner]), both, NN)
+
+    def arrive(tile):
+        @pl.when(has_beyond)
+        def _():
+            halo(tile).wait_recv()
+
+    for chunk in range(chunks):
+        project_tiles(outer, chunk, outer_halo, arrive)
+        if chunk == 0:
+            each(inner_sends, "start")
+        each(outer_sends(chunk), "start")
+    each(first_hops, "wait_recv")
+    each(relays, "start")
+    out[outer] = dot3((fh[outer], fl[outer]), both, NN)
+    each(inner_arrivals, "wait_recv")
+    for chunk in range(chunks):
+        each(outer_arrivals(chunk), "wait_recv")
+
+    for g, part, lanes, is_tail in groups:
         lon = half if is_tail else lons
 
         def spread(value):
@@ -243,7 +303,9 @@
         inverse = spread(gain[2 * REACH, part])
         limit = spread(gain[2 * REACH + 1, part])
         for w in range(WINDOW):
-            dir_a[w, :, :lon] = window[w, :, lanes] * inverse
+            field = gather(window, w, g, is_tail)
+            left[w, :, :lon] = field
+            dir_a[w, :, :lon] = field * inverse
         totals = [dir_a[REACH, :, :lon], dir_a[REACH + 1, :, :lon]]
         now, later = dir_a, dir_b
         for k in range(REACH):
@@ -253,9 +315,9 @@
                 sides = now[w - 1, :, :lon] + now[w + 1, :, :lon]
                 mixed = 4.0 * here + sides
                 laplace = shifted(mixed, 1) + shifted(mixed, -1) + (4.0 * sides - 20.0 * here)
-                residual = window[w, :, lanes] - (here - weight[w - 1, :, lanes] * laplace)
+                residual = left[w, :, :lon] - (here - weight[w - 1, :, lanes] * laplace)
                 if k < REACH - 1:
-                    window[w, :, lanes] = residual
+                    left[w, :, :lon] = residual
                 fresh = keep * here + push * residual
                 later[w, :, :lon] = fresh
                 if REACH <= w < REACH + 2:
@@ -263,23 +325,22 @@
             now, later = later, now
         few = tuple(piece[part] for piece in restore_sel)
         for row in range(rows):
-            change = totals[row] - own[row, :, lanes]
+            change = totals[row] - gather(own, row, g, is_tail)
             if is_tail:
                 change = jnp.concatenate(
                     [jnp.where(upper_half, change, 0.0), jnp.where(upper_half, 0.0, change)], axis=1)
             out[row] += dot3(split(change), few, TN)
 
-    @pl.when(has_north)
+    @pl.when(has_beyond)
     def _():
-        halo(0).wait_send()
-
-    @pl.when(has_south)
-    def _():
-        halo(1).wait_send()
-    for start, sent in [entry[:2] for entry in sends]:
-        @pl.when(sent)
-        def _(start=start):
-            start().wait_send()
+        for tile in range(tiles):
+            halo(tile).wait_send()
+
+    between.wait_send()
+    each(inner_sends, "wait_send")
+    each(relays, "wait_send")
+    for chunk in range(chunks):
+        each(outer_sends(chunk), "wait_send")
 
 
 def solution(mesh):
@@ -294,6 +355,8 @@
         full += 1 if rest and not tail else 0
         ranks = 8 * (full + tail)
         packed = full * lons + tail * lons // 2
+        tiles = lons // 128
+        copies = 9 + 7 * (tiles // 2)
         anywhere = pl.BlockSpec(memory_space=pl.ANY)
         vmem = pltpu.VMEM
         block = vmem((rows, lons, levels), f32)
@@ -309,12 +372,12 @@
                 vmem(mode_slots.shape[::-1], jnp.int32),
                 vmem((lons, levels), f32), vmem((lons, levels), f32),
                 vmem((rows, 8, packed), f32), vmem((WINDOW, 8, packed), f32),
-                vmem((WINDOW, 8, lons), f32), vmem((WINDOW, 8, lons), f32),
+                vmem((WINDOW, 8, lons), f32), vmem((WINDOW, 8, lons), f32), vmem((WINDOW, 8, lons), f32),
                 vmem((WINDOW - 2, 8, packed), f32), vmem((2 * REACH + 2, ranks, 128), f32),
                 vmem((rows, lons, levels), bf16), vmem((rows, lons, levels), bf16),
                 pltpu.SemaphoreType.DMA((9,)),
-                pltpu.SemaphoreType.DMA((2,)), pltpu.SemaphoreType.DMA((2,)),
-                pltpu.SemaphoreType.DMA((9,)), pltpu.SemaphoreType.DMA((9,)),
+                pltpu.SemaphoreType.DMA((tiles + 1,)), pltpu.SemaphoreType.DMA((tiles + 1,)),
+                pltpu.SemaphoreType.DMA((copies,)), pltpu.SemaphoreType.DMA((copies,)),
             ],
             compiler_params=pltpu.CompilerParams(
                 collective_id=0, has_side_effects=True, vmem_limit_bytes=VMEM_LIMIT),

time: 18.8 us -> 18.3 us (0.973)
  Pallas kernels: 17.8 us -> 17.4 us
    pallas_call x1, Pallas kernels: 17.8 us -> 17.4 us  [local(): pl.pallas_call(functools.partial(kernel, devices, full, tail), out_shape=...]
where the time goes in v2:
time: 18.3 us; the launch traced here: 18.2 us
  Pallas kernels  17.4 us (95%)
  local copies, waits for them, and re-layouts  0.8 us (4%)
    pallas_call x1, Pallas kernels, local(): pl.pallas_call(functools.partial(kernel, devices, full, tail), out_shape=...  17.4 us
    unnamed x1, local copies, waits for them, and re-layouts  0.8 us

profile of v2, /device:TPU:0, one launch (start us, length us, event | category | flops | bytes accessed | tf_op | source)
XLA Modules:
  0.0 18.2 jit_solution(14170158471292894699)
XLA Ops:
  0.0 17.4 %shard_map.91 = f32[2,512,128]{2,1,0:T(8,128)S(1)} custom-call(f32[2,512,128]{2,1,0:T(8,128)} %state.1, f32[2,512,128]{2,1,0:T(8,128)} %east_wind.1, f32[2,512,128]{2,1,0:T(8,128)} %north_wind.1, f32[32,512]{1,0:T(8,128)} %coef.1, f32[128,128]{1,0:T(8,128)} %project.1, f32[128,128]{1,0:T(8,128)} %restore.1, f32[1,128]{1,0:T(1,128)} %bitcast.4, ...), custom_call_target="tpu_custom_call" | custom-call | tf_op jit(solution)/shard_map/pallas_call | solution.py:363
  17.4 0.8 %copy.11 = f32[2,512,128]{2,1,0:T(8,128)} copy(f32[2,512,128]{2,1,0:T(8,128)S(1)} %shard_map.91) | data formatting | bytes 1048576

commit v3 on v2

--- a/solution.py
+++ b/solution.py
@@ -39,7 +39,7 @@
 
 def kernel(devices, full, tail, state, east_wind, north_wind, coef, project, restore, stiffness, sweeps,
            mode_slots, out, sv, ev, nv, cv, pv, rv, stv, swv, msv, outer_halo, inner_halo, own, window, dir_a,
-           dir_b, left, weight, gain, fh, fl, load_sem, halo_send, halo_recv, mode_send, mode_recv):
+           dir_b, left, delta, weight, heavy, gain, fh, fl, load_sem, halo_send, halo_recv, mode_send, mode_recv):
     me = lax.axis_index("lat")
     rows, lons, levels = state.shape
     nlat = coef.shape[0]
@@ -177,9 +177,11 @@
         line = cv[pl.ds(jnp.clip(at, 0, nlat - 1), 1), :] * inside
         for _, part, lanes, is_tail in groups:
             if is_tail:
-                weight[w - 1, :, lanes] = sixth[part] * jnp.where(upper_half, line[:, :half], line[:, half:])
+                factor = sixth[part] * jnp.where(upper_half, line[:, :half], line[:, half:])
             else:
-                weight[w - 1, :, lanes] = sixth[part] * line
+                factor = sixth[part] * line
+            weight[w - 1, :, lanes] = factor
+            heavy[w - 1, :, lanes] = 1.0 + 36.0 * factor
 
     def copy(send, recv, source, row, first, size, w, target):
         lanes = pl.ds(first, size)
@@ -310,26 +312,33 @@
         now, later = dir_a, dir_b
         for k in range(REACH):
             keep, push = spread(gain[2 * k, part]), spread(gain[2 * k + 1, part])
+            before, here = now[k, :, :lon], now[k + 1, :, :lon]
             for w in range(k + 1, WINDOW - 1 - k):
-                here = now[w, :, :lon]
-                sides = now[w - 1, :, :lon] + now[w + 1, :, :lon]
-                mixed = 4.0 * here + sides
-                laplace = shifted(mixed, 1) + shifted(mixed, -1) + (4.0 * sides - 20.0 * here)
-                residual = left[w, :, :lon] - (here - weight[w - 1, :, lanes] * laplace)
+                after = now[w + 1, :, :lon]
+                mixed = 4.0 * here + (before + after)
+                around = shifted(mixed, 1) + shifted(mixed, -1) + 4.0 * mixed
+                residual = (left[w, :, :lon] - heavy[w - 1, :, lanes] * here) + weight[w - 1, :, lanes] * around
                 if k < REACH - 1:
                     left[w, :, :lon] = residual
                 fresh = keep * here + push * residual
-                later[w, :, :lon] = fresh
+                if k < REACH - 1:
+                    later[w, :, :lon] = fresh
                 if REACH <= w < REACH + 2:
                     totals[w - REACH] += jnp.where(k + 1 < limit, fresh, 0.0)
+                before, here = here, after
             now, later = later, now
-        few = tuple(piece[part] for piece in restore_sel)
         for row in range(rows):
             change = totals[row] - gather(own, row, g, is_tail)
             if is_tail:
                 change = jnp.concatenate(
                     [jnp.where(upper_half, change, 0.0), jnp.where(upper_half, 0.0, change)], axis=1)
-            out[row] += dot3(split(change), few, TN)
+            delta[row, part] = change
+
+    few = jnp.concatenate([restore_sel[0], restore_sel[1], restore_sel[0]], axis=0)
+    for row in range(rows):
+        high, low = split(delta[row])
+        out[row] += lax.dot_general(
+            jnp.concatenate([high, high, low], axis=0), few, TN, preferred_element_type=f32)
 
     @pl.when(has_beyond)
     def _():
@@ -373,6 +382,7 @@
                 vmem((lons, levels), f32), vmem((lons, levels), f32),
                 vmem((rows, 8, packed), f32), vmem((WINDOW, 8, packed), f32),
                 vmem((WINDOW, 8, lons), f32), vmem((WINDOW, 8, lons), f32), vmem((WINDOW, 8, lons), f32),
+                vmem((rows, ranks, lons), f32), vmem((WINDOW - 2, 8, packed), f32),
                 vmem((WINDOW - 2, 8, packed), f32), vmem((2 * REACH + 2, ranks, 128), f32),
                 vmem((rows, lons, levels), bf16), vmem((rows, lons, levels), bf16),
                 pltpu.SemaphoreType.DMA((9,)),

time: 18.3 us -> 18 us (0.984)
  Pallas kernels: 17.4 us -> 17 us
    pallas_call x1, Pallas kernels: 17.4 us -> 17 us  [local(): pl.pallas_call(functools.partial(kernel, devices, full, tail), out_shape=...]
where the time goes in v3:
time: 18 us; the launch traced here: 17.8 us
  Pallas kernels  17 us (94%)
  local copies, waits for them, and re-layouts  0.8 us (4%)
    pallas_call x1, Pallas kernels, local(): pl.pallas_call(functools.partial(kernel, devices, full, tail), out_shape=...  17 us
    unnamed x1, local copies, waits for them, and re-layouts  0.8 us

profile of v3, /device:TPU:0, one launch (start us, length us, event | category | flops | bytes accessed | tf_op | source)
XLA Modules:
  0.0 17.8 jit_solution(17004458945447835527)
XLA Ops:
  0.0 17.0 %shard_map.91 = f32[2,512,128]{2,1,0:T(8,128)S(1)} custom-call(f32[2,512,128]{2,1,0:T(8,128)} %state.1, f32[2,512,128]{2,1,0:T(8,128)} %east_wind.1, f32[2,512,128]{2,1,0:T(8,128)} %north_wind.1, f32[32,512]{1,0:T(8,128)} %coef.1, f32[128,128]{1,0:T(8,128)} %project.1, f32[128,128]{1,0:T(8,128)} %restore.1, f32[1,128]{1,0:T(1,128)} %bitcast.4, ...), custom_call_target="tpu_custom_call" | custom-call | tf_op jit(solution)/shard_map/pallas_call | solution.py:372
  17.0 0.8 %copy.11 = f32[2,512,128]{2,1,0:T(8,128)} copy(f32[2,512,128]{2,1,0:T(8,128)S(1)} %shard_map.91) | data formatting | bytes 1048576

commit v4 on v3

--- a/solution.py
+++ b/solution.py
@@ -193,9 +193,9 @@
     def whole(send, recv, w, target, source=own, row=inner):
         return lambda: copy(send, recv, source, row, 0, packed, w, target)
 
-    def piece(chunk, send, recv, w, target):
+    def piece(chunk, send, recv, w, target, source=own, row=outer):
         base = 9 + 7 * chunk
-        return lambda: copy(base + send, base + recv, own, outer, chunk * width, width, w, target)
+        return lambda: copy(base + send, base + recv, source, row, chunk * width, width, w, target)
 
     inner_sends = (
         (whole(1, 1, 4 - core, me + 2), high1),
@@ -225,6 +225,14 @@
     def outer_sends(chunk):
         far, far_w = me - 4 + 7 * core, 15 - 13 * core
         far_on = (is1 & high2) | (is0 & low2)
+        if chunk < chunks - 1:
+            return (
+                (piece(chunk, 1, 1 + core, 3 + core, me + 2), high1),
+                (piece(chunk, 3, 3 + core, 11 + core, me - 2), low1),
+                (piece(chunk, 5, 6 - core, far_w, far), far_on),
+                (piece(chunk, 6, 6 - core, far_w - 2, far + 1), far_on),
+                (piece(chunk, 0, 0, 5 + 5 * core, sibling), always),
+            )
         return tuple(
             entry for to in range(2) for entry in (
                 (piece(chunk, 1 + to, 1 + core, 3 + 3 * core - 2 * to, me - core + 2 + to), high1),
@@ -232,7 +240,26 @@
                 (piece(chunk, 5 + to, 6 - core, far_w - 2 * to, far + to), far_on),
             )) + ((piece(chunk, 0, 0, 5 + 5 * core, sibling), always),)
 
+    outer_hops = tuple(
+        entry for chunk in range(chunks - 1) for entry in (
+            (piece(chunk, 1, 1 + core, 3 + core, sibling), low1),
+            (piece(chunk, 3, 3 + core, 11 + core, sibling), high1),
+        ))
+    outer_relays = tuple(
+        entry for chunk in range(chunks - 1) for entry in (
+            (piece(chunk, 2, 1 + core, 1 + 5 * core, sibling, window, 3 + core), low1),
+            (piece(chunk, 4, 3 + core, 9 + 5 * core, sibling, window, 11 + core), high1),
+        ))
+
     def outer_arrivals(chunk):
+        if chunk < chunks - 1:
+            return (
+                (piece(chunk, 1, 2 - core, 6 - 5 * core, sibling), low1),
+                (piece(chunk, 3, 4 - core, 14 - 5 * core, sibling), high1),
+                (piece(chunk, 0, 0, 10 - 5 * core, sibling), always),
+                (piece(chunk, 5, 5, 2 - 2 * core, sibling), low2),
+                (piece(chunk, 6, 6, 15 - 2 * core, sibling), high2),
+            )
         return tuple(
             entry for by in range(2) for entry in (
                 (piece(chunk, 1 + by, 1 + by, 3 + 3 * by - 2 * core, sibling), low1),
@@ -285,6 +312,8 @@
     each(first_hops, "wait_recv")
     each(relays, "start")
     out[outer] = dot3((fh[outer], fl[outer]), both, NN)
+    each(outer_hops, "wait_recv")
+    each(outer_relays, "start")
     each(inner_arrivals, "wait_recv")
     for chunk in range(chunks):
         each(outer_arrivals(chunk), "wait_recv")
@@ -306,23 +335,23 @@
         limit = spread(gain[2 * REACH + 1, part])
         for w in range(WINDOW):
             field = gather(window, w, g, is_tail)
-            left[w, :, :lon] = field
-            dir_a[w, :, :lon] = field * inverse
-        totals = [dir_a[REACH, :, :lon], dir_a[REACH + 1, :, :lon]]
+            left[w, :, lanes] = field
+            dir_a[w, :, lanes] = field * inverse
+        totals = [dir_a[REACH, :, lanes], dir_a[REACH + 1, :, lanes]]
         now, later = dir_a, dir_b
         for k in range(REACH):
             keep, push = spread(gain[2 * k, part]), spread(gain[2 * k + 1, part])
-            before, here = now[k, :, :lon], now[k + 1, :, :lon]
+            before, here = now[k, :, lanes], now[k + 1, :, lanes]
             for w in range(k + 1, WINDOW - 1 - k):
-                after = now[w + 1, :, :lon]
+                after = now[w + 1, :, lanes]
                 mixed = 4.0 * here + (before + after)
                 around = shifted(mixed, 1) + shifted(mixed, -1) + 4.0 * mixed
-                residual = (left[w, :, :lon] - heavy[w - 1, :, lanes] * here) + weight[w - 1, :, lanes] * around
+                residual = (left[w, :, lanes] - heavy[w - 1, :, lanes] * here) + weight[w - 1, :, lanes] * around
                 if k < REACH - 1:
-                    left[w, :, :lon] = residual
+                    left[w, :, lanes] = residual
                 fresh = keep * here + push * residual
                 if k < REACH - 1:
-                    later[w, :, :lon] = fresh
+                    later[w, :, lanes] = fresh
                 if REACH <= w < REACH + 2:
                     totals[w - REACH] += jnp.where(k + 1 < limit, fresh, 0.0)
                 before, here = here, after
@@ -348,6 +377,7 @@
     between.wait_send()
     each(inner_sends, "wait_send")
     each(relays, "wait_send")
+    each(outer_relays, "wait_send")
     for chunk in range(chunks):
         each(outer_sends(chunk), "wait_send")
 
@@ -381,7 +411,8 @@
                 vmem(mode_slots.shape[::-1], jnp.int32),
                 vmem((lons, levels), f32), vmem((lons, levels), f32),
                 vmem((rows, 8, packed), f32), vmem((WINDOW, 8, packed), f32),
-                vmem((WINDOW, 8, lons), f32), vmem((WINDOW, 8, lons), f32), vmem((WINDOW, 8, lons), f32),
+                vmem((WINDOW, 8, packed), f32), vmem((WINDOW, 8, packed), f32),
+                vmem((WINDOW, 8, packed), f32),
                 vmem((rows, ranks, lons), f32), vmem((WINDOW - 2, 8, packed), f32),
                 vmem((WINDOW - 2, 8, packed), f32), vmem((2 * REACH + 2, ranks, 128), f32),
                 vmem((rows, lons, levels), bf16), vmem((rows, lons, levels), bf16),

time: 18 us -> 17.7 us (0.983)
  Pallas kernels: 17 us -> 16.8 us
    pallas_call x1, Pallas kernels: 17 us -> 16.8 us  [local(): pl.pallas_call(functools.partial(kernel, devices, full, tail), out_shape=...]
where the time goes in v4:
time: 17.7 us; the launch traced here: 17.6 us
  Pallas kernels  16.8 us (95%)
  local copies, waits for them, and re-layouts  0.8 us (5%)
    pallas_call x1, Pallas kernels, local(): pl.pallas_call(functools.partial(kernel, devices, full, tail), out_shape=...  16.8 us
    unnamed x1, local copies, waits for them, and re-layouts  0.8 us

profile of v4, /device:TPU:0, one launch (start us, length us, event | category | flops | bytes accessed | tf_op | source)
XLA Modules:
  0.0 17.6 jit_solution(14101712782013934078)
XLA Ops:
  0.0 16.8 %shard_map.91 = f32[2,512,128]{2,1,0:T(8,128)S(1)} custom-call(f32[2,512,128]{2,1,0:T(8,128)} %state.1, f32[2,512,128]{2,1,0:T(8,128)} %east_wind.1, f32[2,512,128]{2,1,0:T(8,128)} %north_wind.1, f32[32,512]{1,0:T(8,128)} %coef.1, f32[128,128]{1,0:T(8,128)} %project.1, f32[128,128]{1,0:T(8,128)} %restore.1, f32[1,128]{1,0:T(1,128)} %bitcast.4, ...), custom_call_target="tpu_custom_call" | custom-call | tf_op jit(solution)/shard_map/pallas_call | solution.py:402
  16.8 0.8 %copy.11 = f32[2,512,128]{2,1,0:T(8,128)} copy(f32[2,512,128]{2,1,0:T(8,128)S(1)} %shard_map.91) | data formatting | bytes 1048576

commit v5 on v4

--- a/solution.py
+++ b/solution.py
@@ -18,7 +18,6 @@
 
 REACH = sweep_limit - 1
 WINDOW = 2 * REACH + 2
-OFFSETS = (1, -1, 2, -2, 3, -3, 4, -4)
 VMEM_LIMIT = 60 * 1024 * 1024
 
 NN = (((1,), (0,)), ((), ()))
@@ -38,8 +37,8 @@
 
 
 def kernel(devices, full, tail, state, east_wind, north_wind, coef, project, restore, stiffness, sweeps,
-           mode_slots, out, sv, ev, nv, cv, pv, rv, stv, swv, msv, outer_halo, inner_halo, own, window, dir_a,
-           dir_b, left, delta, weight, heavy, gain, fh, fl, load_sem, halo_send, halo_recv, mode_send, mode_recv):
+           mode_slots, out, sv, ev, nv, cv, pv, rv, stv, swv, msv, outer_halo, inner_halo, given, kept, own, window, dir_a,
+           dir_b, left, delta, weight, heavy, gain, load_sem, halo_send, halo_recv, mode_send, mode_recv, knock):
     me = lax.axis_index("lat")
     rows, lons, levels = state.shape
     nlat = coef.shape[0]
@@ -56,37 +55,55 @@
     loads = [
         pltpu.make_async_copy(source, target, load_sem.at[i])
         for i, (source, target) in enumerate((
-            (state, sv), (east_wind, ev), (north_wind, nv), (project, pv), (restore, rv),
+            (state, sv.at[pl.ds(0, rows)]), (east_wind, ev.at[pl.ds(0, rows)]), (north_wind, nv.at[pl.ds(0, rows)]),
+            (project, pv), (restore, rv),
             (mode_slots, msv), (stiffness, stv), (sweeps, swv), (coef, cv)))
     ]
     for load in loads:
         load.start()
 
     barrier = pltpu.get_barrier_semaphore()
-    for offset in OFFSETS:
-        @pl.when((me + offset >= 0) & (me + offset < devices))
-        def _(offset=offset):
-            pl.semaphore_signal(barrier, inc=1, device_id={"lat": me + offset}, device_id_type=MESH)
-    pl.semaphore_wait(barrier, jnp.minimum(me, 4) + jnp.minimum(devices - 1 - me, 4))
-
     low1, low2, high1, high2 = chip >= 1, chip >= 2, chip + 1 < chips, chip + 2 < chips
     is0, is1 = core == 0, core == 1
     always = me >= 0
     sibling = me + 1 - 2 * core
-    beyond = me - 1 + 2 * core
+    beyond = me - 1 + 3 * core
     has_beyond = (is0 & low1) | (is1 & high1)
 
-    def halo(tile):
+    def signal(semaphore, target, on):
+        @pl.when(on)
+        def _():
+            pl.semaphore_signal(semaphore, inc=1, device_id={"lat": target}, device_id_type=MESH)
+
+    def hear(semaphore, on):
+        @pl.when(on)
+        def _():
+            pl.semaphore_wait(semaphore, 1)
+
+    signal(barrier, sibling, always)
+    signal(barrier, me - 2, is1 & low1)
+    signal(barrier, me + 1, is1 & high1)
+    pl.semaphore_wait(barrier, 1 + has_beyond.astype(jnp.int32))
+
+    def halo(tile, kind=inner):
+        span, slot = pl.ds(tile * 128, 128), kind * tiles + tile
+        return pltpu.make_async_remote_copy(
+            src_ref=state.at[outer, span], dst_ref=outer_halo.at[kind, span],
+            send_sem=halo_send.at[tile], recv_sem=halo_recv.at[slot],
+            device_id={"lat": beyond}, device_id_type=MESH)
+
+    def beside(source, target, slot):
+        return pltpu.make_async_remote_copy(
+            src_ref=source, dst_ref=target, send_sem=halo_send.at[slot], recv_sem=halo_recv.at[slot],
+            device_id={"lat": sibling}, device_id_type=MESH)
+
+    between = beside(state.at[inner], inner_halo, 2 * tiles)
+    lent = [beside(source.at[0], target.at[rows], 2 * tiles + 1 + i) for i, (source, target) in enumerate(
+        ((state, sv), (east_wind, ev), (north_wind, nv)))]
+
+    def give(tile):
         span = pl.ds(tile * 128, 128)
-        return pltpu.make_async_remote_copy(
-            src_ref=state.at[outer, span], dst_ref=outer_halo.at[span],
-            send_sem=halo_send.at[tile], recv_sem=halo_recv.at[tile],
-            device_id={"lat": beyond}, device_id_type=MESH)
-
-    between = pltpu.make_async_remote_copy(
-        src_ref=state.at[inner], dst_ref=inner_halo,
-        send_sem=halo_send.at[tiles], recv_sem=halo_recv.at[tiles],
-        device_id={"lat": sibling}, device_id_type=MESH)
+        return beside(given.at[0, span], given.at[0, span], 2 * tiles + 4 + tile)
 
     @pl.when(has_beyond)
     def _():
@@ -96,9 +113,21 @@
 
     between.start()
 
-    @pl.when(jnp.logical_not(has_beyond))
-    def _():
-        outer_halo[...] = jnp.zeros_like(outer_halo)
+    @pl.when(is0)
+    def _():
+        for copy in lent:
+            copy.start()
+
+    signal(knock.at[0], me + 2, is1 & high1)
+    signal(knock.at[1], me - 1, is0 & low1)
+
+    @pl.when(jnp.logical_not(low1))
+    def _():
+        outer_halo[0] = jnp.zeros(outer_halo.shape[1:], f32)
+
+    @pl.when(jnp.logical_not(high1))
+    def _():
+        outer_halo[1] = jnp.zeros(outer_halo.shape[1:], f32)
 
     for w in range(WINDOW):
         at = 2 * me - REACH + w
@@ -110,14 +139,21 @@
     for load in loads[:3]:
         load.wait()
     sign0 = (0.5 * time_step) * (2 * core - 1).astype(f32)
-    for row, sign in ((inner, sign0), (outer, -sign0)):
-        here, other = sv[row], sv[1 - row]
+
+    def prepare(row, sign, other):
+        here = sv[row]
         east = pltpu.roll(here, lons - 1, 0)
         west = pltpu.roll(here, 1, 0)
         wind = nv[row] * sign
         ev[row] = (here - (0.5 * time_step) * ev[row] * (east - west) - wind * other
                    + (time_step * diffusion) * (east + west + other - 4.0 * here))
         nv[row] = wind + time_step * diffusion
+
+    prepare(inner, sign0, sv[outer])
+
+    @pl.when(is1)
+    def _():
+        prepare(1, -sign0, sv[0])
 
     for load in loads[3:]:
         load.wait()
@@ -193,8 +229,8 @@
     def whole(send, recv, w, target, source=own, row=inner):
         return lambda: copy(send, recv, source, row, 0, packed, w, target)
 
-    def piece(chunk, send, recv, w, target, source=own, row=outer):
-        base = 9 + 7 * chunk
+    def piece(chunk, send, recv, w, target, source=own, row=0):
+        base = 9 + 14 * chunk
         return lambda: copy(base + send, base + recv, source, row, chunk * width, width, w, target)
 
     inner_sends = (
@@ -222,53 +258,43 @@
         (whole(8, 8, 13 - 3 * core, sibling), high1),
     )
 
-    def outer_sends(chunk):
-        far, far_w = me - 4 + 7 * core, 15 - 13 * core
-        far_on = (is1 & high2) | (is0 & low2)
-        if chunk < chunks - 1:
-            return (
-                (piece(chunk, 1, 1 + core, 3 + core, me + 2), high1),
-                (piece(chunk, 3, 3 + core, 11 + core, me - 2), low1),
-                (piece(chunk, 5, 6 - core, far_w, far), far_on),
-                (piece(chunk, 6, 6 - core, far_w - 2, far + 1), far_on),
-                (piece(chunk, 0, 0, 5 + 5 * core, sibling), always),
-            )
+    def outer_sends(chunk, kind):
+        row, first, recv = 2 - kind, 7 * kind, 4 * kind
+        far_on = is1 & (((kind == 0) & low2) | ((kind == 1) & high2))
+        cores = range(2) if chunk == chunks - 1 else (1,)
+        near = tuple(
+            entry for to in cores for entry in (
+                (piece(chunk, first + 3 + to, recv + 2, 11 + 3 * kind - 2 * to, me - 3 + to, own, row), is1 & low1),
+                (piece(chunk, first + 1 + to, recv + 1, 3 + 3 * kind - 2 * to, me + 1 + to, own, row), is1 & high1),
+            ))
+        far = tuple(
+            (piece(chunk, first + 5 + to, recv + 3, 15 - 13 * kind - 2 * to, me - 5 + 8 * kind + to, own, row), far_on)
+            for to in range(2))
+        return near + far + ((piece(chunk, first, recv, 7 + 3 * kind, sibling, own, row), is1),)
+
+    def near_arrivals(chunk, on):
         return tuple(
-            entry for to in range(2) for entry in (
-                (piece(chunk, 1 + to, 1 + core, 3 + 3 * core - 2 * to, me - core + 2 + to), high1),
-                (piece(chunk, 3 + to, 3 + core, 11 + 3 * core - 2 * to, me - core - 2 + to), low1),
-                (piece(chunk, 5 + to, 6 - core, far_w - 2 * to, far + to), far_on),
-            )) + ((piece(chunk, 0, 0, 5 + 5 * core, sibling), always),)
-
-    outer_hops = tuple(
-        entry for chunk in range(chunks - 1) for entry in (
-            (piece(chunk, 1, 1 + core, 3 + core, sibling), low1),
-            (piece(chunk, 3, 3 + core, 11 + core, sibling), high1),
+            entry for kind in range(2) for entry in (
+                (piece(chunk, 7 * kind + 1, 4 * kind + 1, 3 + 3 * kind - 2 * core, sibling), on & low1),
+                (piece(chunk, 7 * kind + 3, 4 * kind + 2, 11 + 3 * kind - 2 * core, sibling), on & high1),
+            ))
+
+    def other_arrivals(chunk):
+        return (
+            (piece(chunk, 5, 3, 15 - 2 * core, sibling), high2),
+            (piece(chunk, 12, 7, 2 - 2 * core, sibling), low2),
+            (piece(chunk, 0, 0, 7, sibling), is0),
+            (piece(chunk, 7, 4, 10, sibling), is0),
+        )
+
+    early = lax.rem(chip, 2)
+    kinds = (early, 1 - early)
+    outer_hops = tuple(entry for chunk in range(chunks - 1) for entry in near_arrivals(chunk, is1))
+    outer_relays = tuple(
+        entry for chunk in range(chunks - 1) for kind in range(2) for entry in (
+            (piece(chunk, 7 * kind + 1, 4 * kind + 1, 3 + 3 * kind, sibling, window, 1 + 3 * kind), is1 & low1),
+            (piece(chunk, 7 * kind + 3, 4 * kind + 2, 11 + 3 * kind, sibling, window, 9 + 3 * kind), is1 & high1),
         ))
-    outer_relays = tuple(
-        entry for chunk in range(chunks - 1) for entry in (
-            (piece(chunk, 2, 1 + core, 1 + 5 * core, sibling, window, 3 + core), low1),
-            (piece(chunk, 4, 3 + core, 9 + 5 * core, sibling, window, 11 + core), high1),
-        ))
-
-    def outer_arrivals(chunk):
-        if chunk < chunks - 1:
-            return (
-                (piece(chunk, 1, 2 - core, 6 - 5 * core, sibling), low1),
-                (piece(chunk, 3, 4 - core, 14 - 5 * core, sibling), high1),
-                (piece(chunk, 0, 0, 10 - 5 * core, sibling), always),
-                (piece(chunk, 5, 5, 2 - 2 * core, sibling), low2),
-                (piece(chunk, 6, 6, 15 - 2 * core, sibling), high2),
-            )
-        return tuple(
-            entry for by in range(2) for entry in (
-                (piece(chunk, 1 + by, 1 + by, 3 + 3 * by - 2 * core, sibling), low1),
-                (piece(chunk, 3 + by, 3 + by, 11 + 3 * by - 2 * core, sibling), high1),
-            )) + (
-                (piece(chunk, 0, 0, 10 - 5 * core, sibling), always),
-                (piece(chunk, 5, 5, 2 - 2 * core, sibling), low2),
-                (piece(chunk, 6, 6, 15 - 2 * core, sibling), high2),
-            )
 
     def each(entries, action):
         for make, on in entries:
@@ -276,47 +302,89 @@
             def _(make=make):
                 getattr(make(), action)()
 
-    def project_tiles(row, chunk, halo_ref, ready):
+    def project_tiles(row, chunk, halo_of, ready, keep, slot, w):
         found = []
         for tile in (chunk, chunk + chunks):
             ready(tile)
             span = pl.ds(tile * 128, 128)
-            forcing = ev[row, span] + nv[row, span] * halo_ref[span]
-            pieces = split(forcing)
-            fh[row, span], fl[row, span] = pieces
-            found.append(dot3(project_sel, pieces, NT))
+            forcing = ev[row, span] + nv[row, span] * halo_of(span)
+            keep(tile, span, forcing)
+            found.append(dot3(project_sel, split(forcing), NT))
         for g, part, _, is_tail in groups:
             if is_tail:
                 fields = ((chunk, jnp.where(upper_tile, found[0][part], found[1][part])),)
             else:
                 fields = ((chunk, found[0][part]), (chunk + chunks, found[1][part]))
             for tile, field in fields:
-                own[row, :, place_of(g, tile)] = field
-                window[REACH + row, :, place_of(g, tile)] = field
+                own[slot, :, place_of(g, tile)] = field
+                window[w, :, place_of(g, tile)] = field
+
+    def keep_inner(tile, span, forcing):
+        kept[span] = forcing
 
     between.wait_recv()
     for chunk in range(chunks):
-        project_tiles(inner, chunk, inner_halo, lambda tile: None)
-    out[inner] = dot3((fh[inner], fl[inner]), both, NN)
-
-    def arrive(tile):
-        @pl.when(has_beyond)
+        project_tiles(inner, chunk, lambda span: inner_halo[span], lambda tile: None, keep_inner, inner,
+                      REACH + inner)
+    out[inner] = dot3(split(kept[...]), both, NN)
+
+    hear(knock.at[0], is1 & low1)
+    hear(knock.at[1], is1 & high1)
+    signal(knock.at[2], me + 2, is1 & high1)
+    signal(knock.at[3], me - 2, is1 & low1)
+    hear(knock.at[2], is1 & low1)
+    hear(knock.at[3], is1 & high1)
+    signal(knock.at[4], sibling, is1)
+    hear(knock.at[4], is0)
+
+    @pl.when(is0)
+    def _():
+        @pl.when(low1)
         def _():
-            halo(tile).wait_recv()
-
-    for chunk in range(chunks):
-        project_tiles(outer, chunk, outer_halo, arrive)
-        if chunk == 0:
-            each(inner_sends, "start")
-        each(outer_sends(chunk), "start")
-    each(first_hops, "wait_recv")
-    each(relays, "start")
-    out[outer] = dot3((fh[outer], fl[outer]), both, NN)
+            pass
+
+        each(inner_sends, "start")
+        each(first_hops, "wait_recv")
+        each(relays, "start")
+        for tile in range(tiles):
+            give(tile).wait_recv()
+
+    @pl.when(is1)
+    def _():
+        for copy in lent:
+            copy.wait_recv()
+        prepare(rows, 0.5 * time_step, inner_halo[...])
+        for kind in kinds:
+            def arrive(tile, kind=kind):
+                @pl.when(((kind == 0) & low1) | ((kind == 1) & high1))
+                def _():
+                    halo(tile, kind).wait_recv()
+
+            def keep(tile, span, forcing, kind=kind):
+                given[kind, span] = forcing
+
+            for chunk in range(chunks):
+                project_tiles(2 - kind, chunk, lambda span, kind=kind: outer_halo[kind, span], arrive, keep,
+                              2 - kind, 5 + 3 * kind)
+                each(outer_sends(chunk, kind), "start")
+
+            @pl.when(kind == 0)
+            def _():
+                for tile in range(tiles):
+                    give(tile).start()
+
+            if kind is kinds[0]:
+                each(inner_sends, "start")
+        each(first_hops, "wait_recv")
+        each(relays, "start")
+
+    out[outer] = dot3(split(given[outer]), both, NN)
     each(outer_hops, "wait_recv")
     each(outer_relays, "start")
     each(inner_arrivals, "wait_recv")
     for chunk in range(chunks):
-        each(outer_arrivals(chunk), "wait_recv")
+        each(near_arrivals(chunk, always if chunk == chunks - 1 else is0), "wait_recv")
+        each(other_arrivals(chunk), "wait_recv")
 
     for g, part, lanes, is_tail in groups:
         lon = half if is_tail else lons
@@ -357,7 +425,7 @@
                 before, here = here, after
             now, later = later, now
         for row in range(rows):
-            change = totals[row] - gather(own, row, g, is_tail)
+            change = totals[row] - gather(window, REACH + row, g, is_tail)
             if is_tail:
                 change = jnp.concatenate(
                     [jnp.where(upper_half, change, 0.0), jnp.where(upper_half, 0.0, change)], axis=1)
@@ -371,15 +439,28 @@
 
     @pl.when(has_beyond)
     def _():
+        for chunk in range(0, chunks):
+            halo(chunk).wait_send()
+            halo(chunk + chunks).wait_send()
+
+    between.wait_send()
+
+    @pl.when(is0)
+    def _():
+        for copy in lent:
+            copy.wait_send()
+
+    @pl.when(is1)
+    def _():
         for tile in range(tiles):
-            halo(tile).wait_send()
-
-    between.wait_send()
+            give(tile).wait_send()
+
     each(inner_sends, "wait_send")
     each(relays, "wait_send")
     each(outer_relays, "wait_send")
-    for chunk in range(chunks):
-        each(outer_sends(chunk), "wait_send")
+    for kind in kinds:
+        for chunk in range(chunks):
+            each(outer_sends(chunk, kind), "wait_send")
 
 
 def solution(mesh):
@@ -395,10 +476,10 @@
         ranks = 8 * (full + tail)
         packed = full * lons + tail * lons // 2
         tiles = lons // 128
-        copies = 9 + 7 * (tiles // 2)
+        copies = 9 + 14 * (tiles // 2)
         anywhere = pl.BlockSpec(memory_space=pl.ANY)
         vmem = pltpu.VMEM
-        block = vmem((rows, lons, levels), f32)
+        block = vmem((rows + 1, lons, levels), f32)
         return pl.pallas_call(
             functools.partial(kernel, devices, full, tail),
             out_shape=pltpu.VMEM(state.shape, f32),
@@ -409,16 +490,17 @@
                 vmem(coef.shape, f32), vmem(project.shape, f32), vmem(restore.shape, f32),
                 vmem((1, levels), f32), vmem((1, levels), jnp.int32),
                 vmem(mode_slots.shape[::-1], jnp.int32),
-                vmem((lons, levels), f32), vmem((lons, levels), f32),
-                vmem((rows, 8, packed), f32), vmem((WINDOW, 8, packed), f32),
+                vmem((2, lons, levels), f32), vmem((lons, levels), f32), vmem((2, lons, levels), f32),
+                vmem((lons, levels), f32),
+                vmem((rows + 1, 8, packed), f32), vmem((WINDOW, 8, packed), f32),
                 vmem((WINDOW, 8, packed), f32), vmem((WINDOW, 8, packed), f32),
                 vmem((WINDOW, 8, packed), f32),
                 vmem((rows, ranks, lons), f32), vmem((WINDOW - 2, 8, packed), f32),
                 vmem((WINDOW - 2, 8, packed), f32), vmem((2 * REACH + 2, ranks, 128), f32),
-                vmem((rows, lons, levels), bf16), vmem((rows, lons, levels), bf16),
                 pltpu.SemaphoreType.DMA((9,)),
-                pltpu.SemaphoreType.DMA((tiles + 1,)), pltpu.SemaphoreType.DMA((tiles + 1,)),
+                pltpu.SemaphoreType.DMA((3 * tiles + 4,)), pltpu.SemaphoreType.DMA((3 * tiles + 4,)),
                 pltpu.SemaphoreType.DMA((copies,)), pltpu.SemaphoreType.DMA((copies,)),
+                pltpu.SemaphoreType.REGULAR((5,)),
             ],
             compiler_params=pltpu.CompilerParams(
                 collective_id=0, has_side_effects=True, vmem_limit_bytes=VMEM_LIMIT),

time: 17.7 us -> 17.3 us (0.977)
  the two profiles are of different devices: /device:TPU:0 before, /device:TPU:23 now
where the time goes in v5:
time: 17.3 us; the launch traced here: 17.2 us
  Pallas kernels  16.3 us (94%)
  local copies, waits for them, and re-layouts  0.8 us (5%)
    pallas_call x1, Pallas kernels, local(): pl.pallas_call(functools.partial(kernel, devices, full, tail), out_shape=...  16.3 us
    unnamed x1, local copies, waits for them, and re-layouts  0.8 us

profile of v5, /device:TPU:23, one launch (start us, length us, event | category | flops | bytes accessed | tf_op | source)
XLA Modules:
  0.0 17.2 jit_solution(17426306910188765866)
XLA Ops:
  0.0 16.3 %shard_map.91 = f32[2,512,128]{2,1,0:T(8,128)S(1)} custom-call(f32[2,512,128]{2,1,0:T(8,128)} %state.1, f32[2,512,128]{2,1,0:T(8,128)} %east_wind.1, f32[2,512,128]{2,1,0:T(8,128)} %north_wind.1, f32[32,512]{1,0:T(8,128)} %coef.1, f32[128,128]{1,0:T(8,128)} %project.1, f32[128,128]{1,0:T(8,128)} %restore.1, f32[1,128]{1,0:T(1,128)} %bitcast.4, ...), custom_call_target="tpu_custom_call" | custom-call | tf_op jit(solution)/shard_map/pallas_call | solution.py:483
  16.4 0.8 %copy.11 = f32[2,512,128]{2,1,0:T(8,128)} copy(f32[2,512,128]{2,1,0:T(8,128)S(1)} %shard_map.91) | data formatting | bytes 1048576

commit v6 on v5

--- a/solution.py
+++ b/solution.py
@@ -105,9 +105,17 @@
         span = pl.ds(tile * 128, 128)
         return beside(given.at[0, span], given.at[0, span], 2 * tiles + 4 + tile)
 
+    held = has_beyond & (is0 & (chip == chips - 2))
+    swift = has_beyond & jnp.logical_not(is0 & (chip == chips - 2))
+
     @pl.when(has_beyond)
     def _():
-        for chunk in range(chunks):
+        halo(0).start()
+        halo(chunks).start()
+
+    @pl.when(swift)
+    def _():
+        for chunk in range(1, chunks):
             halo(chunk).start()
             halo(chunk + chunks).start()
 
@@ -150,6 +158,19 @@
         nv[row] = wind + time_step * diffusion
 
     prepare(inner, sign0, sv[outer])
+
+    @pl.when(held)
+    def _():
+        halo(0).wait_send()
+        halo(chunks).wait_send()
+        for chunk in range(1, chunks):
+            halo(chunk).start()
+            halo(chunk + chunks).start()
+
+    hear(knock.at[0], is1 & low1)
+    hear(knock.at[1], is1 & high1)
+    signal(knock.at[2], me + 2, is1 & high1)
+    signal(knock.at[3], me - 2, is1 & low1)
 
     @pl.when(is1)
     def _():
@@ -328,10 +349,6 @@
                       REACH + inner)
     out[inner] = dot3(split(kept[...]), both, NN)
 
-    hear(knock.at[0], is1 & low1)
-    hear(knock.at[1], is1 & high1)
-    signal(knock.at[2], me + 2, is1 & high1)
-    signal(knock.at[3], me - 2, is1 & low1)
     hear(knock.at[2], is1 & low1)
     hear(knock.at[3], is1 & high1)
     signal(knock.at[4], sibling, is1)
@@ -437,9 +454,14 @@
         out[row] += lax.dot_general(
             jnp.concatenate([high, high, low], axis=0), few, TN, preferred_element_type=f32)
 
+    @pl.when(swift)
+    def _():
+        halo(0).wait_send()
+        halo(chunks).wait_send()
+
     @pl.when(has_beyond)
     def _():
-        for chunk in range(0, chunks):
+        for chunk in range(1, chunks):
             halo(chunk).wait_send()
             halo(chunk + chunks).wait_send()
 

time: 17.3 us -> 16.6 us (0.960)
  the two profiles are of different devices: /device:TPU:23 before, /device:TPU:0 now
where the time goes in v6:
time: 16.6 us; the launch traced here: 16.5 us
  Pallas kernels  15.7 us (95%)
  local copies, waits for them, and re-layouts  0.8 us (5%)
    pallas_call x1, Pallas kernels, local(): pl.pallas_call(functools.partial(kernel, devices, full, tail), out_shape=...  15.7 us
    unnamed x1, local copies, waits for them, and re-layouts  0.8 us

profile of v6, /device:TPU:0, one launch (start us, length us, event | category | flops | bytes accessed | tf_op | source)
XLA Modules:
  0.0 16.5 jit_solution(7160814327287373010)
XLA Ops:
  0.0 15.7 %shard_map.91 = f32[2,512,128]{2,1,0:T(8,128)S(1)} custom-call(f32[2,512,128]{2,1,0:T(8,128)} %state.1, f32[2,512,128]{2,1,0:T(8,128)} %east_wind.1, f32[2,512,128]{2,1,0:T(8,128)} %north_wind.1, f32[32,512]{1,0:T(8,128)} %coef.1, f32[128,128]{1,0:T(8,128)} %project.1, f32[128,128]{1,0:T(8,128)} %restore.1, f32[1,128]{1,0:T(1,128)} %bitcast.4, ...), custom_call_target="tpu_custom_call" | custom-call | tf_op jit(solution)/shard_map/pallas_call | solution.py:505
  15.7 0.8 %copy.11 = f32[2,512,128]{2,1,0:T(8,128)} copy(f32[2,512,128]{2,1,0:T(8,128)S(1)} %shard_map.91) | data formatting | bytes 1048576

commit v7 on v6

--- a/solution.py
+++ b/solution.py
@@ -105,8 +105,8 @@
         span = pl.ds(tile * 128, 128)
         return beside(given.at[0, span], given.at[0, span], 2 * tiles + 4 + tile)
 
-    held = has_beyond & (is0 & (chip == chips - 2))
-    swift = has_beyond & jnp.logical_not(is0 & (chip == chips - 2))
+    held = has_beyond & ((is1 & (lax.rem(chip, 2) == 1)) | (is0 & (chip == chips - 2)))
+    swift = has_beyond & jnp.logical_not((is1 & (lax.rem(chip, 2) == 1)) | (is0 & (chip == chips - 2)))
 
     @pl.when(has_beyond)
     def _():

time: 16.6 us -> 16.6 us (level)
  the two profiles are of different devices: /device:TPU:0 before, /device:TPU:21 now
where the time goes in v7:
time: 16.6 us; the launch traced here: 16.5 us
  Pallas kernels  15.7 us (95%)
  local copies, waits for them, and re-layouts  0.8 us (5%)
    pallas_call x1, Pallas kernels, local(): pl.pallas_call(functools.partial(kernel, devices, full, tail), out_shape=...  15.7 us
    unnamed x1, local copies, waits for them, and re-layouts  0.8 us

profile of v7, /device:TPU:21, one launch (start us, length us, event | category | flops | bytes accessed | tf_op | source)
XLA Modules:
  0.0 16.5 jit_solution(15940280453838240091)
XLA Ops:
  0.0 15.7 %shard_map.91 = f32[2,512,128]{2,1,0:T(8,128)S(1)} custom-call(f32[2,512,128]{2,1,0:T(8,128)} %state.1, f32[2,512,128]{2,1,0:T(8,128)} %east_wind.1, f32[2,512,128]{2,1,0:T(8,128)} %north_wind.1, f32[32,512]{1,0:T(8,128)} %coef.1, f32[128,128]{1,0:T(8,128)} %project.1, f32[128,128]{1,0:T(8,128)} %restore.1, f32[1,128]{1,0:T(1,128)} %bitcast.4, ...), custom_call_target="tpu_custom_call" | custom-call | tf_op jit(solution)/shard_map/pallas_call | solution.py:505
  15.7 0.8 %copy.11 = f32[2,512,128]{2,1,0:T(8,128)} copy(f32[2,512,128]{2,1,0:T(8,128)S(1)} %shard_map.91) | data formatting | bytes 1048576
